TPU v7x, 32 devices: a whole 2x2x4 slice. The times are simulated.
32 devices in a mesh: dp: 2 (over y), seq: 16 (over z, x, core).
Axes of the slice: x: 2, y: 2, z: 4, core: 2. Of those that a mesh axis runs over, the one named last changes fastest.
Arguments:
- tokens: bfloat16 [2, 4096, 4096], P('dp', 'seq'), may hold values from -6 to 6
- queries: bfloat16 [2, 4096, 128], P('dp', 'seq'), may hold values from -6 to 6
- key_vectors: bfloat16 [2, 4096, 128], P('dp', 'seq'), may hold values from -6 to 6
- doc_position: int32 [2, 4096], P('dp', 'seq'), may hold values from 0 to 4095, as said below
- value_scores: float32 [2, 4096, 4], P('dp', 'seq'), may hold values from 0.1 to 1
- value_experts: int32 [2, 4096, 2], P('dp', 'seq'), may hold values from 0 to 3, all different within a row
- output_scores: float32 [2, 4096, 4], P('dp', 'seq'), may hold values from 0.1 to 1
- output_experts: int32 [2, 4096, 2], P('dp', 'seq'), may hold values from 0 to 3, all different within a row
- value_panels: bfloat16 [4096, 512], P('seq'), may hold values from -0.09375 to 0.09375
- output_panels: bfloat16 [4096, 512], P('seq'), may hold values from -3 to 3
- cotangent: bfloat16 [2, 4096, 4096], P('dp', 'seq'), may hold values from -0.4375 to 0.4375
Outputs:
- layer_output: bfloat16 [2, 4096, 4096], P('dp', 'seq')
- grad_tokens: bfloat16 [2, 4096, 4096], P('dp', 'seq')
- grad_queries: bfloat16 [2, 4096, 128], P('dp', 'seq')
- grad_keys: bfloat16 [2, 4096, 128], P('dp', 'seq')
- grad_value: float32 [4096, 512], P('seq')
- grad_output: float32 [4096, 512], P('seq')
Inputs may be any that keep to these rules, and one draw needn't show every extreme that they name: doc_position[b, i] is i minus the first position of the document that holds position i; position 0 starts a document in every sequence; sequence 0 is one document; every other sequence holds one to four documents.
All inputs are finite; a program needn't handle non-finite values.
Results may differ from a plain program's by a relative error of at most 0.035.
Values may be sent and summed in bfloat16 or wider, within the bound.
A program may use at most 128 MiB of HBM per device.

v0:
```python
import jax
import jax.numpy as jnp
from jax import lax
from jax.sharding import PartitionSpec as P


def expert_gates(scores, chosen, experts):
    chosen_hit = chosen[:, :, None] == lax.iota(jnp.int32, experts)[None, None, :]
    return jnp.where(jnp.any(chosen_hit, axis=1), scores, jnp.float32(0.0))


def contract_last(left, right):
    return lax.dot_general(
        left, right, (((1,), (1,)), ((), ())), preferred_element_type=jnp.float32
    )


def contract_first(left, right):
    return lax.dot_general(
        left, right, (((0,), (0,)), ((), ())), preferred_element_type=jnp.float32
    )


def body(
    tokens,
    queries,
    key_vectors,
    doc_position,
    value_scores,
    value_experts,
    output_scores,
    output_experts,
    value_panels,
    output_panels,
    cotangent,
):
    tok_block = tokens[0]
    query_block = queries[0]
    own_keys = key_vectors[0]
    positions = doc_position[0]
    grad_rows = cotangent[0]
    tok_rows = tok_block.shape[0]
    head_size = query_block.shape[1]
    experts = value_scores.shape[2]
    panel_width = value_panels.shape[1]
    value_gate = expert_gates(value_scores[0], value_experts[0], experts)
    output_gate = expert_gates(output_scores[0], output_experts[0], experts)
    value_full, output_full = (
        lax.all_gather(value_panels, "seq", axis=0, tiled=True),
        lax.all_gather(output_panels, "seq", axis=0, tiled=True),
    )
    projection = jnp.dot(tok_block, value_full, preferred_element_type=jnp.float32)
    value_vec = jnp.sum(
        projection.reshape(tok_rows, experts, head_size) * value_gate[:, :, None], axis=1
    ).astype(jnp.bfloat16)
    keys_all, values_all = (
        lax.all_gather(own_keys, "seq", axis=0, tiled=True),
        lax.all_gather(value_vec, "seq", axis=0, tiled=True),
    )
    length = keys_all.shape[0]
    score_scale = head_size ** (-0.5)
    query_index = lax.axis_index("seq") * tok_rows + lax.iota(jnp.int32, tok_rows)
    key_index = lax.iota(jnp.int32, length)
    visible = (key_index[None, :] <= query_index[:, None]) & (
        query_index[:, None] - key_index[None, :] <= positions[:, None]
    )
    masked = jnp.where(visible, contract_last(query_block, keys_all) * score_scale, -jnp.inf)
    row_max = jnp.max(masked, axis=1)
    log_total = row_max + jnp.log(jnp.sum(jnp.exp(masked - row_max[:, None]), axis=1))
    attn_prob = jnp.exp(masked - log_total[:, None])
    prob_low = attn_prob.astype(jnp.bfloat16)
    attended = jnp.dot(prob_low, values_all, preferred_element_type=jnp.float32).astype(
        jnp.bfloat16
    )
    expanded = (
        (output_gate[:, :, None] * attended.astype(jnp.float32)[:, None, :])
        .reshape(tok_rows, panel_width)
        .astype(jnp.bfloat16)
    )
    layer_output = contract_last(expanded, output_full).astype(jnp.bfloat16)
    pulled = jnp.dot(grad_rows, output_full, preferred_element_type=jnp.float32)
    dattended = jnp.sum(
        pulled.reshape(tok_rows, experts, head_size) * output_gate[:, :, None], axis=1
    ).astype(jnp.bfloat16)
    row_delta = jnp.sum(dattended.astype(jnp.float32) * attended.astype(jnp.float32), axis=1)
    dweights = contract_last(dattended, values_all)
    dscores = (attn_prob * (dweights - row_delta[:, None])).astype(jnp.bfloat16)
    grad_queries = (
        jnp.dot(dscores, keys_all, preferred_element_type=jnp.float32) * score_scale
    ).astype(jnp.bfloat16)
    key_term = contract_first(dscores, query_block) * score_scale
    value_term = contract_first(prob_low, dattended)
    dkey_sum, dvalue_sum = (
        lax.psum_scatter(
            key_term.astype(jnp.bfloat16), "seq", scatter_dimension=0, tiled=True
        ).astype(jnp.float32),
        lax.psum_scatter(
            value_term.astype(jnp.bfloat16), "seq", scatter_dimension=0, tiled=True
        ).astype(jnp.float32),
    )
    grad_keys = dkey_sum.astype(jnp.bfloat16)
    dvalue = dvalue_sum.astype(jnp.bfloat16)
    value_grad = (
        (value_gate[:, :, None] * dvalue.astype(jnp.float32)[:, None, :])
        .reshape(tok_rows, panel_width)
        .astype(jnp.bfloat16)
    )
    grad_tokens = contract_last(value_grad, value_full).astype(jnp.bfloat16)
    term_value = contract_first(tok_block, value_grad)
    term_output = contract_first(grad_rows, expanded)
    owned = lax.psum_scatter(
        jnp.concatenate([term_value, term_output], axis=1).astype(jnp.bfloat16),
        "seq",
        scatter_dimension=0,
        tiled=True,
    )
    summed = lax.psum(owned, "dp").astype(jnp.float32)
    return (
        layer_output[None],
        grad_tokens[None],
        grad_queries[None],
        grad_keys[None],
        summed[:, :panel_width],
        summed[:, panel_width:],
    )


def solution(mesh):
    in_specs = (
        P("dp", "seq", None),
        P("dp", "seq", None),
        P("dp", "seq", None),
        P("dp", "seq"),
        P("dp", "seq", None),
        P("dp", "seq", None),
        P("dp", "seq", None),
        P("dp", "seq", None),
        P("seq", None),
        P("seq", None),
        P("dp", "seq", None),
    )
    out_specs = (
        P("dp", "seq", None),
        P("dp", "seq", None),
        P("dp", "seq", None),
        P("dp", "seq", None),
        P("seq", None),
        P("seq", None),
    )
    return jax.shard_map(body, mesh=mesh, in_specs=in_specs, out_specs=out_specs, check_vma=False)
```

profile of v0, /device:TPU:0, one launch (start us, length us, event | category | flops | bytes accessed | tf_op | source)
XLA Modules:
  0.0 473.3 jit_solution(2682005454198461691)
XLA Ops:
  7.2 0.0 copy-start
  7.2 0.0 all-gather.12.cloned.1.call-start
  7.2 0.7 all-gather.12.cloned.1.call-update
  7.9 0.0 all-gather.10.cloned.1.call-start
  8.0 0.7 all-gather.10.cloned.1.call-update
  8.7 0.0 all-gather.6.cloned.1.call-start
  8.7 0.7 all-gather.6.cloned.1.call-update
  9.4 0.0 reduce-scatter.4.cloned.1.call-start
  9.5 0.7 fusion.35
  10.2 0.7 bitcast_select_fusion.1
  10.9 40.0 %all-gather.12.cloned.1.call-done = bf16[1,4096,128]{2,1,0:T(8,128)(2,1)} async-done(((bf16[1,256,128]{2,1,0:T(8,128)(2,1)}), bf16[1,4096,128]{2,1,0:T(8,128)(2,1)}) %all-gather.12.cloned.1.call-update) | async-done | bytes 1048592 | tf_op jit(solution)/shard_map/all_gather | solution.py:57
  50.8 2.8 fusion.42
  53.7 1.9 copy-done.1
  55.6 0.7 exponential_reduce_fusion
  56.3 46.2 %all-gather.10.cloned.1.call-done = bf16[4096,512]{1,0:T(8,128)(2,1)} async-done(((bf16[256,512]{1,0:T(8,128)(2,1)}), bf16[4096,512]{1,0:T(8,128)(2,1)}) %all-gather.10.cloned.1.call-update) | async-done | bytes 4194320 | tf_op jit(solution)/shard_map/all_gather | solution.py:50
  102.5 6.4 %copy.46 = bf16[512,4096]{1,0:T(8,128)(2,1)} copy(bf16[512,4096]{0,1:T(8,128)(2,1)} %bitcast.72) | data formatting | bytes 8388608 | tf_op jit(solution)/shard_map/dot_general | solution.py:81
  109.0 4.3 fusion.22
  113.3 0.0 copy-start.11
  113.3 0.0 copy-start.10
  113.3 0.1 copy.47
  113.4 4.2 convolution_convert_fusion.4
  117.6 0.0 reduce-scatter.4.cloned.1.call-update
  117.6 0.0 all-gather.8.cloned.1.call-start
  117.7 0.0 copy-done.10
  117.7 36.1 %all-gather.6.cloned.1.call-done = bf16[4096,512]{1,0:T(8,128)(2,1)} async-done(((bf16[256,512]{1,0:T(8,128)(2,1)}), bf16[4096,512]{1,0:T(8,128)(2,1)}) %all-gather.6.cloned.1.call-update) | async-done | bytes 4194320 | tf_op jit(solution)/shard_map/all_gather | solution.py:49
  153.8 6.4 %copy.43 = bf16[512,4096]{1,0:T(8,128)(2,1)} copy(bf16[512,4096]{0,1:T(8,128)(2,1)} %bitcast.73) | data formatting | bytes 8388608 | tf_op jit(solution)/shard_map/dot_general | solution.py:52
  160.2 4.2 fusion.25
  164.4 0.0 all-gather.8.cloned.1.call-update
  164.4 0.0 reduce-scatter.8.cloned.1.call-start
  164.5 49.3 %reduce-scatter.4.cloned.1.call-done = bf16[256,128]{1,0:T(8,128)(2,1)} async-done(((bf16[4096,128]{1,0:T(8,128)(2,1)}), bf16[256,128]{1,0:T(8,128)(2,1)}) %reduce-scatter.4.cloned.1.call-update) | async-done | bytes 65552 | tf_op jit(solution)/shard_map/reduce_scatter | solution.py:97
  213.7 0.8 convert_element_type.83
  214.6 0.2 multiply_convert_fusion
  214.8 0.1 copy.48
  214.9 3.2 fusion
  218.2 35.4 %all-gather.8.cloned.1.call-done = bf16[4096,128]{1,0:T(8,128)(2,1)} async-done(((bf16[256,128]{1,0:T(8,128)(2,1)}), bf16[4096,128]{1,0:T(8,128)(2,1)}) %all-gather.8.cloned.1.call-update) | async-done | bytes 1048592 | tf_op jit(solution)/shard_map/all_gather | solution.py:58
  253.6 3.5 multiply_reduce_fusion
  257.0 0.1 copy.44
  257.1 0.2 multiply_convert_fusion.1
  257.3 0.1 copy.45
  257.5 0.0 copy-start.6
  257.5 4.9 %fusion.1 = bf16[4096,512]{0,1:T(8,128)(2,1)} fusion(bf16[256,512]{0,1:T(8,128)(2,1)S(1)} %bitcast.78, bf16[1,256,4096]{2,1,0:T(8,128)(2,1)} %param.21), kind=kOutput, calls=%fused_computation.4 | convolution fusion | flops 1075838976 | bytes 6553600 | tf_op jit(solution)/shard_map/dot_general | solution.py:19
  262.4 7.8 %pad_maximum_fusion = bf16[4096,1024]{0,1:T(8,128)(2,1)} fusion(bf16[4096,512]{0,1:T(8,128)(2,1)} %fusion.1, bf16[4096,512]{0,1:T(8,128)(2,1)} %fusion), kind=kLoop, calls=%fused_computation | loop fusion | flops 16777216 | bytes 16777216 | tf_op jit(solution)/shard_map/concatenate | solution.py:112
  270.2 0.0 reduce-scatter.8.cloned.1.call-update
  270.3 0.0 copy-start.9
  270.3 0.0 all-reduce.2.cloned.1.call-start
  270.3 103.8 %reduce-scatter.8.cloned.1.call-done = bf16[256,1024]{0,1:T(8,128)(2,1)} async-done(((bf16[4096,1024]{0,1:T(8,128)(2,1)}), bf16[256,1024]{0,1:T(8,128)(2,1)}) %reduce-scatter.8.cloned.1.call-update) | async-done | bytes 524304 | tf_op jit(solution)/shard_map/reduce_scatter | solution.py:111
  374.2 0.0 all-reduce.2.cloned.1.call-update
  374.2 0.2 reduce-scatter.6.cloned.1.call-start
  374.4 0.0 copy-done.5
  374.4 3.4 fusion.4
  377.8 0.0 copy-start.2
  377.8 1.3 copy-done.2
  379.1 1.7 fusion.7
  380.9 0.0 reduce-scatter.6.cloned.1.call-update
  380.9 0.0 copy-start.3
  380.9 0.0 copy-start.7
  380.9 5.0 %fusion.6 = bf16[1,256,4096]{2,1,0:T(8,128)(2,1)} fusion(bf16[256,512]{0,1:T(8,128)(2,1)S(1)} %bitcast.77, bf16[4096,512]{1,0:T(8,128)(2,1)} %all-gather.6.cloned.1.call-done), kind=kOutput, calls=%fused_computation.13 | convolution fusion | flops 1074790400 | bytes 6553600 | tf_op jit(solution)/shard_map/dot_general | solution.py:13
  386.0 1.3 fusion.30
  387.3 2.6 fusion.5
  390.0 14.9 %all-reduce.2.cloned.1.call-done = bf16[256,1024]{0,1:T(8,128)(2,1)} async-done(((bf16[256,1024]{0,1:T(8,128)(2,1)}), bf16[256,1024]{0,1:T(8,128)(2,1)}) %all-reduce.2.cloned.1.call-update) | async-done | bytes 524304 | tf_op jit(solution)/shard_map/psum | solution.py:117
  404.9 1.1 fusion.41
  406.0 1.0 copy.50
  407.0 1.0 copy.49
  408.0 58.5 %reduce-scatter.6.cloned.1.call-done = bf16[256,128]{1,0:T(8,128)(2,1)} async-done(((bf16[4096,128]{1,0:T(8,128)(2,1)}), bf16[256,128]{1,0:T(8,128)(2,1)}) %reduce-scatter.6.cloned.1.call-update) | async-done | bytes 65552 | tf_op jit(solution)/shard_map/reduce_scatter | solution.py:94
  (16 shorter events, 0.1 us)
Async XLA Ops:
  7.2 153.0 %copy-start = (bf16[1,256,4096]{2,1,0:T(8,128)(2,1)S(1)}, bf16[1,256,4096]{2,1,0:T(8,128)(2,1)}, u32[]{:S(2)}) copy-start(bf16[1,256,4096]{2,1,0:T(8,128)(2,1)} %param.11) | copy-start | bytes 6291460
  7.2 43.7 %all-gather.12.cloned.1.call-start = ((), (), s32[]{:S(2)}) async-start(), calls=%async_computation.10 | async-start | bytes 1114112 | tf_op jit(solution)/shard_map/all_gather | solution.py:57
  7.9 94.6 %all-gather.10.cloned.1.call-start = ((), (), s32[]{:S(2)}) async-start(), calls=%async_computation.5 | async-start | bytes 4456448 | tf_op jit(solution)/shard_map/all_gather | solution.py:50
  8.7 145.1 %all-gather.6.cloned.1.call-start = ((), (), s32[]{:S(2)}) async-start(), calls=%async_computation.3 | async-start | bytes 4456448 | tf_op jit(solution)/shard_map/all_gather | solution.py:49
  9.4 204.3 %reduce-scatter.4.cloned.1.call-start = ((), (), s32[]{:S(2)}) async-start(), calls=%async_computation.6 | async-start | bytes 1114112 | tf_op jit(solution)/shard_map/reduce_scatter | solution.py:97
  53.6 1.9 copy-start.1
  113.3 4.4 copy-start.11
  113.3 4.4 copy-start.10
  117.6 136.0 %all-gather.8.cloned.1.call-start = ((), (), s32[]{:S(2)}) async-start(), calls=%async_computation.4 | async-start | bytes 1114112 | tf_op jit(solution)/shard_map/all_gather | solution.py:58
  164.4 209.7 %reduce-scatter.8.cloned.1.call-start = ((), (), s32[]{:S(2)}) async-start(), calls=%async_computation.8 | async-start | bytes 8912896 | tf_op jit(solution)/shard_map/reduce_scatter | solution.py:111
  257.5 12.7 %copy-start.6 = (bf16[256,4,128]{0,2,1:T(8,128)(2,1)}, bf16[256,4,128]{0,2,1:T(8,128)(2,1)S(1)}, u32[]{:S(2)}) copy-start(bf16[256,4,128]{0,2,1:T(8,128)(2,1)S(1)} %copy.45) | copy-start | bytes 786436
  270.2 104.2 %copy-start.5 = (bf16[4096,128]{1,0:T(8,128)(2,1)S(1)}, bf16[4096,128]{1,0:T(8,128)(2,1)}, u32[]{:S(2)}) copy-start(bf16[4096,128]{1,0:T(8,128)(2,1)} %all-gather.8.cloned.1.call-done) | copy-start | bytes 3145732
  270.3 108.9 %copy-start.9 = (bf16[1,256,128]{2,1,0:T(8,128)(2,1)S(1)}, bf16[1,256,128]{2,1,0:T(8,128)(2,1)}, u32[]{:S(2)}) copy-start(bf16[1,256,128]{2,1,0:T(8,128)(2,1)} %param.12) | copy-start | bytes 196612
  270.3 134.7 %all-reduce.2.cloned.1.call-start = ((), (), s32[]{:S(2)}) async-start(), calls=%async_computation.9 | async-start | bytes 1048576 | tf_op jit(solution)/shard_map/psum | solution.py:117
  374.2 92.3 %reduce-scatter.6.cloned.1.call-start = ((), (), s32[]{:S(2)}) async-start(), calls=%async_computation.7 | async-start | bytes 1114112 | tf_op jit(solution)/shard_map/reduce_scatter | solution.py:94
  377.8 1.3 copy-start.2
  380.9 5.1 %copy-start.8 = (bf16[1,4096,128]{2,1,0:T(8,128)(2,1)S(1)}, bf16[1,4096,128]{2,1,0:T(8,128)(2,1)}, u32[]{:S(2)}) copy-start(bf16[1,4096,128]{2,1,0:T(8,128)(2,1)} %all-gather.12.cloned.1.call-done) | copy-start | bytes 3145732
  380.9 5.1 %copy-start.3 = (bf16[256,4096]{1,0:T(8,128)(2,1)S(1)}, bf16[256,4096]{1,0:T(8,128)(2,1)}, u32[]{:S(2)}) copy-start(bf16[256,4096]{1,0:T(8,128)(2,1)} %copy-done.2) | copy-start | bytes 6291460
  380.9 6.4 %copy-start.4 = (bf16[4096,512]{1,0:T(8,128)(2,1)S(1)}, bf16[4096,512]{1,0:T(8,128)(2,1)}, u32[]{:S(2)}) copy-start(bf16[4096,512]{1,0:T(8,128)(2,1)} %all-gather.10.cloned.1.call-done) | copy-start | bytes 12582916
  380.9 6.4 %copy-start.7 = (bf16[256,4,128]{0,2,1:T(8,128)(2,1)S(1)}, bf16[256,4,128]{0,2,1:T(8,128)(2,1)}, u32[]{:S(2)}) copy-start(bf16[256,4,128]{0,2,1:T(8,128)(2,1)} %copy-done.6) | copy-start | bytes 786436
Sparse Core Ops, SparseCore 0:
  10.2 40.6 all-gather.11
  53.0 49.4 all-gather.9
  104.7 49.0 all-gather.5
  157.8 55.8 reduce-scatter.3
  216.5 36.9 all-gather.7
  270.4 103.7 reduce-scatter.7
  376.6 28.3 all-reduce.1
  409.1 57.3 reduce-scatter.5
where the time goes:
time: 474 us; the launch traced here: 473 us
  waiting for transfers between devices  386 us (81%)
  matrix products  41.2 us (9%)
  local copies, waits for them, and re-layouts  19.8 us (4%)
  between operations  14.3 us (3%)
  other arithmetic  11.2 us (2%)
    reduce_scatter x1, waiting for transfers between devices, body(): lax.psum_scatter(jnp.concatenate([term_value, term_output], axis=1).astyp...  104 us
    reduce_scatter x1, waiting for transfers between devices, body(): lax.psum_scatter(key_term.astype(jnp.bfloat16), 'seq', scatter_dimension=...  58.5 us
    reduce_scatter x1, waiting for transfers between devices, body(): lax.psum_scatter(value_term.astype(jnp.bfloat16), 'seq', scatter_dimensio...  49.3 us
    all_gather x1, waiting for transfers between devices, body(): lax.all_gather(output_panels, 'seq', axis=0, tiled=True)  46.2 us
    all_gather x1, waiting for transfers between devices, body(): lax.all_gather(own_keys, 'seq', axis=0, tiled=True)  40 us
    all_gather x1, waiting for transfers between devices, body(): lax.all_gather(value_panels, 'seq', axis=0, tiled=True)  36.1 us
    all_gather x1, waiting for transfers between devices, body(): lax.all_gather(value_vec, 'seq', axis=0, tiled=True)  35.4 us
    psum x1, waiting for transfers between devices, body(): summed = lax.psum(owned, 'dp').astype(jnp.float32)  14.9 us
  transfers between devices with their start and end apart: 8, of which 8 were waited for; matrix products, arithmetic and copies ran while one was open for 11% of the time, Pallas kernels for 0%

commit v1 on v0

--- a/solution.py
+++ b/solution.py
@@ -1,7 +1,437 @@
+import functools
+
 import jax
 import jax.numpy as jnp
 from jax import lax
+from jax.experimental import pallas as pl
+from jax.experimental.pallas import tpu as pltpu
 from jax.sharding import PartitionSpec as P
+
+MESH = pl.DeviceIdType.MESH
+
+
+class Place:
+    def __init__(self, lines, crosses):
+        index = lax.axis_index("seq")
+        self.lines, self.crosses = lines, crosses
+        self.dp = lax.axis_index("dp")
+        self.a = index // (2 * crosses)
+        self.b = (index // 2) % crosses
+        self.c = index % 2
+        self.side = self.dp % 2
+        self.mate = self.dp + 1 - 2 * self.side
+
+    def at(self, a=None, b=None, c=None, dp=None):
+        a = self.a if a is None else a
+        b = self.b if b is None else b
+        c = self.c if c is None else c
+        dp = self.dp if dp is None else dp
+        return (dp, (a * self.crosses + b) * 2 + c)
+
+    def others(self):
+        return [lax.rem(self.b + k, self.crosses) for k in range(1, self.crosses)]
+
+    def greet(self, paired):
+        barrier = pltpu.get_barrier_semaphore()
+
+        def hail(device):
+            pl.semaphore_signal(barrier, inc=1, device_id=device, device_id_type=MESH)
+
+        @pl.when(self.a > 0)
+        def _():
+            hail(self.at(a=self.a - 1))
+
+        @pl.when(self.a < self.lines - 1)
+        def _():
+            hail(self.at(a=self.a + 1))
+
+        for q in self.others():
+            hail(self.at(b=q))
+        hail(self.at(c=1 - self.c))
+        if paired:
+            hail(self.at(dp=self.mate))
+
+    def await_greetings(self, paired):
+        barrier = pltpu.get_barrier_semaphore()
+
+        ends = jnp.where(self.a > 0, 1, 0) + jnp.where(self.a < self.lines - 1, 1, 0)
+        pl.semaphore_wait(barrier, ends + self.crosses + (1 if paired else 0))
+
+    def ring(self, t):
+        if t == 0:
+            return [(self.a, 0, None)]
+        up, down = self.a + t, self.a - t
+        return [(down, -1, down >= 0), (up, 1, up < self.lines)]
+
+
+def only(flag, action):
+    if flag is None:
+        action()
+    else:
+        pl.when(flag)(action)
+
+
+def both(left, right):
+    if left is None:
+        return right
+    return left if right is None else jnp.logical_and(left, right)
+
+
+def split_rows(rows):
+    alone = rows * 3 // 8
+    return rows - alone, alone
+
+
+def gather_kernel(lines, crosses, paired, *refs):
+    count = len(paired)
+    owns, outs = refs[:count], refs[count : 2 * count]
+    sems = refs[2 * count : 3 * count]
+    local_sem = refs[3 * count]
+    here = Place(lines, crosses)
+    pieces = lines * crosses
+    zs0, zr0 = 0, 2 * lines
+    xs0 = 3 * lines
+    xr0, ys0, yr0, cs0, cr0 = (xs0 + k * pieces for k in range(1, 6))
+    any_pair = any(paired)
+
+    def span(item, p, q, c, part):
+        rows = owns[item].shape[0]
+        start = ((p * crosses + q) * 2 + c) * rows
+        if part == "whole" or not paired[item]:
+            return outs[item].at[pl.ds(pl.multiple_of(start, 16), rows)]
+        carried, alone = split_rows(rows)
+        if part == "carried":
+            return outs[item].at[
+                pl.ds(pl.multiple_of(start + alone * here.side, 16), carried)
+            ]
+        side = here.side if part == "mine" else 1 - here.side
+        return outs[item].at[
+            pl.ds(pl.multiple_of(start + carried * side, 16), alone)
+        ]
+
+    def move(item, ref, send, recv, device):
+        return pltpu.make_async_remote_copy(
+            src_ref=ref,
+            dst_ref=ref,
+            send_sem=sems[item].at[send],
+            recv_sem=sems[item].at[recv],
+            device_id=device,
+            device_id_type=MESH,
+        )
+
+    def along(item, p, step):
+        return move(
+            item, span(item, p, here.b, here.c, "carried"),
+            zs0 + 2 * p + (1 if step > 0 else 0), zr0 + p, here.at(a=here.a + step),
+        )
+
+    def across(item, p, q):
+        return move(
+            item, span(item, p, here.b, here.c, "carried"),
+            xs0 + p * crosses + q, xr0 + p * crosses + here.b, here.at(b=q),
+        )
+
+    def crossed(item, p, q):
+        return move(
+            item, span(item, p, q, here.c, "carried"),
+            xs0 + p * crosses + q, xr0 + p * crosses + q, here.at(b=q),
+        )
+
+    def to_mate(item, p, q, part="mine"):
+        return move(
+            item, span(item, p, q, here.c, part),
+            ys0 + p * crosses + q, yr0 + p * crosses + q, here.at(dp=here.mate),
+        )
+
+    def to_core(item, p, q, c):
+        return move(
+            item, span(item, p, q, c, "whole"),
+            cs0 + p * crosses + q, cr0 + p * crosses + q, here.at(c=1 - here.c),
+        )
+
+    def pass_on(item, p, q):
+        if paired[item]:
+            to_mate(item, p, q).start()
+        else:
+            to_core(item, p, q, here.c).start()
+
+    here.greet(any_pair)
+    copies = [
+        pltpu.make_async_copy(
+            owns[item], span(item, here.a, here.b, here.c, "whole"), local_sem.at[item]
+        )
+        for item in range(count)
+    ]
+    for copy in copies:
+        copy.start()
+    for copy in copies:
+        copy.wait()
+    here.await_greetings(any_pair)
+
+    up_ok, down_ok = here.a < lines - 1, here.a > 0
+
+    def send_line(item, p, step):
+        only(up_ok if step > 0 else down_ok, lambda: along(item, p, step).start())
+
+    for item in range(count):
+        send_line(item, here.a, 1)
+        send_line(item, here.a, -1)
+        for q in here.others():
+            across(item, here.a, q).start()
+        to_core(item, here.a, here.b, here.c).start()
+
+    def take_across(t):
+        for p, _, ok in here.ring(t):
+
+            def action(p=p):
+                for item in range(count):
+                    for q in here.others():
+                        crossed(item, p, q).wait_recv()
+                        pass_on(item, p, q)
+
+            only(ok, action)
+
+    def take_mate(t):
+        for p, _, ok in here.ring(t):
+
+            def action(p=p):
+                for item in range(count):
+                    if paired[item]:
+                        for q in here.others() + ([] if t == 0 else [here.b]):
+                            to_mate(item, p, q, "theirs").wait_recv()
+                            to_core(item, p, q, here.c).start()
+
+            only(ok, action)
+
+    for t in range(1, lines):
+        for p, step, ok in here.ring(t):
+
+            def action(p=p, step=step):
+                for item in range(count):
+                    along(item, p, -step).wait_recv()
+                    send_line(item, p, -step)
+                    for q in here.others():
+                        across(item, p, q).start()
+                    pass_on(item, p, here.b)
+
+            only(ok, action)
+        take_across(t - 1)
+        if t >= 2:
+            take_mate(t - 2)
+    take_across(lines - 1)
+    if lines >= 2:
+        take_mate(lines - 2)
+    take_mate(lines - 1)
+
+    for p in range(lines):
+        for q in range(crosses):
+            for item in range(count):
+                to_core(item, p, q, 1 - here.c).wait_recv()
+                to_core(item, p, q, here.c).wait_send()
+                if paired[item]:
+                    pl.when(jnp.logical_or(p != here.a, q != here.b))(
+                        lambda item=item, p=p, q=q: to_mate(item, p, q).wait_send()
+                    )
+    for p in range(lines):
+        for item in range(count):
+            for q in here.others():
+                across(item, p, q).wait_send()
+            pl.when(jnp.logical_and(up_ok, p <= here.a))(
+                lambda item=item, p=p: along(item, p, 1).wait_send()
+            )
+            pl.when(jnp.logical_and(down_ok, p >= here.a))(
+                lambda item=item, p=p: along(item, p, -1).wait_send()
+            )
+
+
+def layout(size):
+    lines = 4 if size % 8 == 0 else 1
+    return lines, size // (2 * lines)
+
+
+def gather(arrays, paired, size, collective_id):
+    lines, crosses = layout(size)
+    count = len(arrays)
+    return pl.pallas_call(
+        functools.partial(gather_kernel, lines, crosses, tuple(paired)),
+        out_shape=[
+            jax.ShapeDtypeStruct((size * x.shape[0],) + x.shape[1:], x.dtype) for x in arrays
+        ],
+        in_specs=[pl.BlockSpec(memory_space=pl.ANY)] * count,
+        out_specs=[pl.BlockSpec(memory_space=pl.ANY)] * count,
+        scratch_shapes=[
+            pltpu.SemaphoreType.DMA((3 * lines + 6 * lines * crosses,)) for _ in range(count)
+        ]
+        + [pltpu.SemaphoreType.DMA((count,))],
+        compiler_params=pltpu.CompilerParams(
+            collective_id=collective_id, has_side_effects=True
+        ),
+    )(*arrays)
+
+
+def reduce_kernel(lines, crosses, paired, x_ref, out_ref, total, core_in, mate_in, cross_in,
+                  line_in, last_in, sems):
+    here = Place(lines, crosses)
+    pieces = lines * crosses
+    rows = out_ref.shape[0]
+    carried, alone = split_rows(rows) if paired else (rows, 0)
+    cs0, cr0, ys0, yr0, xs0, xr0 = (k * pieces for k in range(6))
+    zs0 = 6 * pieces
+    zr0, fs, fr = zs0 + lines, zs0 + 3 * lines, zs0 + 3 * lines + 1
+    first = pl.ds(pl.multiple_of(alone * here.side, 16), carried) if paired else pl.ds(0, rows)
+    mine = pl.ds(pl.multiple_of(carried * here.side, 16), alone)
+    theirs = pl.ds(pl.multiple_of(carried * (1 - here.side), 16), alone)
+
+    def move(src, dst, send, recv, device):
+        return pltpu.make_async_remote_copy(
+            src_ref=src, dst_ref=dst, send_sem=sems.at[send], recv_sem=sems.at[recv],
+            device_id=device, device_id_type=MESH,
+        )
+
+    def slot(p, q):
+        return p * crosses + q
+
+    def piece(p, q, c):
+        return pl.ds(pl.multiple_of(((p * crosses + q) * 2 + c) * rows, 16), rows)
+
+    def to_core(p, q):
+        k = slot(p, q)
+        return move(x_ref.at[piece(p, q, 1 - here.c)], core_in.at[k], cs0 + k, cr0 + k,
+                    here.at(c=1 - here.c))
+
+    def to_mate(p, q):
+        k = slot(p, q)
+        return move(total.at[k, theirs], mate_in.at[k], ys0 + k, yr0 + k,
+                    here.at(dp=here.mate))
+
+    def across(p, q):
+        return move(total.at[slot(p, q), first], cross_in.at[slot(p, here.b)],
+                    xs0 + slot(p, q), xr0 + slot(p, here.b), here.at(b=q))
+
+    def crossed(p, q):
+        return move(total.at[slot(p, q), first], cross_in.at[slot(p, q)],
+                    xs0 + slot(p, q), xr0 + slot(p, q), here.at(b=q))
+
+    def along(p, step):
+        k = 2 * p + (0 if step > 0 else 1)
+        return move(total.at[slot(p, here.b), first], line_in.at[k], zs0 + p, zr0 + k,
+                    here.at(a=here.a + step))
+
+    def final():
+        return move(total.at[slot(here.a, here.b), first], last_in, fs, fr,
+                    here.at(dp=here.mate))
+
+    here.greet(paired)
+    here.await_greetings(paired)
+    order = [(t, q) for t in range(lines - 1, -1, -1) for q in here.others() + [here.b]]
+    for t, q in order:
+        for p, _, ok in here.ring(t):
+            only(ok, lambda p=p, q=q: to_core(p, q).start())
+    for t, q in order:
+        for p, _, ok in here.ring(t):
+
+            def join(p=p, q=q):
+                k = slot(p, q)
+                to_core(p, q).wait_recv()
+                total[k] = x_ref[piece(p, q, here.c)] + core_in[k]
+                if paired:
+                    to_mate(p, q).start()
+
+            only(ok, join)
+    for t in range(lines - 1, -1, -1):
+        for q in here.others():
+            for p, _, ok in here.ring(t):
+
+                def cross(p=p, q=q):
+                    k = slot(p, q)
+                    if paired:
+                        to_mate(p, q).wait_recv()
+                        total[k, mine] = total[k, mine] + mate_in[k]
+                    across(p, q).start()
+
+                only(ok, cross)
+        for p, _, ok in here.ring(t):
+
+            def fold(p=p):
+                if paired:
+                    k = slot(p, here.b)
+                    to_mate(p, here.b).wait_recv()
+                    total[k, mine] = total[k, mine] + mate_in[k]
+
+            only(ok, fold)
+    for t in range(lines - 1, -1, -1):
+        for p, step, ok in here.ring(t):
+
+            def run(p=p, step=step):
+                k = slot(p, here.b)
+                for q in here.others():
+                    crossed(p, q).wait_recv()
+                    total[k, first] = total[k, first] + cross_in[slot(p, q)]
+
+                def add(side):
+                    along(p, 1 if side == 0 else -1).wait_recv()
+                    total[k, first] = total[k, first] + line_in[2 * p + side]
+
+                if step >= 0:
+                    pl.when(here.a > 0)(lambda: add(0))
+                if step <= 0:
+                    pl.when(here.a < lines - 1)(lambda: add(1))
+                if step != 0:
+                    along(p, step).start()
+
+            only(ok, run)
+
+    k = slot(here.a, here.b)
+    if paired:
+        final().start()
+        final().wait_recv()
+        out_ref[mine] = total[k, mine].astype(out_ref.dtype)
+        their_at = pl.multiple_of(alone * (1 - here.side) * 0 + (carried - alone) * (1 - here.side), 16)
+        out_ref[theirs] = last_in[pl.ds(their_at, alone)].astype(out_ref.dtype)
+        middle = carried - alone
+        shared_at = pl.multiple_of(alone * here.side, 16)
+        out_ref[pl.ds(alone, middle)] = total[k, pl.ds(alone, middle)].astype(
+            out_ref.dtype
+        ) + last_in[pl.ds(shared_at, middle)].astype(out_ref.dtype)
+        final().wait_send()
+    else:
+        out_ref[...] = total[k].astype(out_ref.dtype)
+    for p in range(lines):
+        for q in range(crosses):
+            to_core(p, q).wait_send()
+            if paired:
+                to_mate(p, q).wait_send()
+        for q in here.others():
+            across(p, q).wait_send()
+        pl.when(p > here.a)(lambda p=p: along(p, 1).wait_send())
+        pl.when(p < here.a)(lambda p=p: along(p, -1).wait_send())
+
+
+def reduce_scatter(x, paired, size, out_dtype, collective_id):
+    lines, crosses = layout(size)
+    pieces = lines * crosses
+    rows, width = x.shape[0] // size, x.shape[1]
+    carried, alone = split_rows(rows) if paired else (rows, 16)
+    kind = x.dtype
+    return pl.pallas_call(
+        functools.partial(reduce_kernel, lines, crosses, paired),
+        out_shape=jax.ShapeDtypeStruct((rows, width), out_dtype),
+        in_specs=[pl.BlockSpec(memory_space=pltpu.VMEM)],
+        out_specs=pl.BlockSpec(memory_space=pltpu.VMEM),
+        scratch_shapes=[
+            pltpu.VMEM((pieces, rows, width), kind),
+            pltpu.VMEM((pieces, rows, width), kind),
+            pltpu.VMEM((pieces, alone, width), kind),
+            pltpu.VMEM((pieces, carried, width), kind),
+            pltpu.VMEM((2 * lines, carried, width), kind),
+            pltpu.VMEM((carried, width), kind),
+            pltpu.SemaphoreType.DMA((6 * pieces + 3 * lines + 2,)),
+        ],
+        compiler_params=pltpu.CompilerParams(
+            collective_id=collective_id, has_side_effects=True,
+            vmem_limit_bytes=56 * 1024 * 1024,
+        ),
+    )(x)
 
 
 def expert_gates(scores, chosen, experts):
@@ -45,18 +475,16 @@
     panel_width = value_panels.shape[1]
     value_gate = expert_gates(value_scores[0], value_experts[0], experts)
     output_gate = expert_gates(output_scores[0], output_experts[0], experts)
-    value_full, output_full = (
-        lax.all_gather(value_panels, "seq", axis=0, tiled=True),
-        lax.all_gather(output_panels, "seq", axis=0, tiled=True),
+    size = lax.axis_size("seq")
+    pair_count = lax.axis_size("dp")
+    keys_all, value_full, output_full = gather(
+        [own_keys, value_panels, output_panels], [False, True, True], size, 0
     )
     projection = jnp.dot(tok_block, value_full, preferred_element_type=jnp.float32)
     value_vec = jnp.sum(
         projection.reshape(tok_rows, experts, head_size) * value_gate[:, :, None], axis=1
     ).astype(jnp.bfloat16)
-    keys_all, values_all = (
-        lax.all_gather(own_keys, "seq", axis=0, tiled=True),
-        lax.all_gather(value_vec, "seq", axis=0, tiled=True),
-    )
+    (values_all,) = gather([value_vec], [False], size, 1)
     length = keys_all.shape[0]
     score_scale = head_size ** (-0.5)
     query_index = lax.axis_index("seq") * tok_rows + lax.iota(jnp.int32, tok_rows)
@@ -90,16 +518,11 @@
     ).astype(jnp.bfloat16)
     key_term = contract_first(dscores, query_block) * score_scale
     value_term = contract_first(prob_low, dattended)
-    dkey_sum, dvalue_sum = (
-        lax.psum_scatter(
-            key_term.astype(jnp.bfloat16), "seq", scatter_dimension=0, tiled=True
-        ).astype(jnp.float32),
-        lax.psum_scatter(
-            value_term.astype(jnp.bfloat16), "seq", scatter_dimension=0, tiled=True
-        ).astype(jnp.float32),
-    )
-    grad_keys = dkey_sum.astype(jnp.bfloat16)
-    dvalue = dvalue_sum.astype(jnp.bfloat16)
+    own_sums = reduce_scatter(
+        jnp.concatenate([key_term, value_term], axis=1).astype(jnp.bfloat16),
+        False, size, jnp.bfloat16, 2,
+    )
+    grad_keys, dvalue = own_sums[:, :head_size], own_sums[:, head_size:]
     value_grad = (
         (value_gate[:, :, None] * dvalue.astype(jnp.float32)[:, None, :])
         .reshape(tok_rows, panel_width)
@@ -108,13 +531,12 @@
     grad_tokens = contract_last(value_grad, value_full).astype(jnp.bfloat16)
     term_value = contract_first(tok_block, value_grad)
     term_output = contract_first(grad_rows, expanded)
-    owned = lax.psum_scatter(
+    summed = reduce_scatter(
         jnp.concatenate([term_value, term_output], axis=1).astype(jnp.bfloat16),
-        "seq",
-        scatter_dimension=0,
-        tiled=True,
-    )
-    summed = lax.psum(owned, "dp").astype(jnp.float32)
+        True, size, jnp.float32, 3,
+    )
+    if pair_count > 2:
+        summed = lax.psum(summed * 0.5, "dp")
     return (
         layer_output[None],
         grad_tokens[None],

time: 474 us -> 237 us (0.50)
  waiting for transfers between devices: 386 us -> 0 us
  Pallas kernels: 0 us -> 188 us
  local copies, waits for them, and re-layouts: 19.8 us -> 4.45 us
  between operations: 14.3 us -> 0.82 us
  matrix products: 41.2 us -> 28.3 us
    reduce_scatter x3 -> x0, waiting for transfers between devices: 212 us -> none  [the longest x1 104 us: body(): lax.psum_scatter(jnp.concatenate([term_value, term_output], axis=1).astyp...]
    pallas_call x0 -> x4, Pallas kernels: none -> 188 us  [the longest x2 103 us: reduce_scatter(): pl.pallas_call(functools.partial(reduce_kernel, lines, crosses, paired),...]
    all_gather x4 -> x0, waiting for transfers between devices: 158 us -> none  [the longest x1 46.2 us: body(): lax.all_gather(output_panels, 'seq', axis=0, tiled=True)]
    psum x1 -> x0, waiting for transfers between devices: 14.9 us -> none  [body(): summed = lax.psum(owned, 'dp').astype(jnp.float32)]
    dot_general x2 -> x0, local copies, waits for them, and re-layouts: 12.9 us -> none  [the longest x1 6.43 us: body(): pulled = jnp.dot(grad_rows, output_full, preferred_element_type=jnp.float32)]
    dot_general x4, matrix products: 14 us -> 7.97 us  [contract_first(): lax.dot_general(left, right, (((0,), (0,)), ((), ())), preferred_element_...]
  transfers between devices with their start and end apart: 8 -> 0, of which waited for: 8 -> 0; matrix products, arithmetic and copies ran while one was open for 11% -> 0% of each run, Pallas kernels for 0% -> 0%
where the time goes in v1:
time: 237 us; the launch traced here: 236 us
  Pallas kernels  188 us (79%)
  matrix products  28.3 us (12%)
  other arithmetic  14.7 us (6%)
  local copies, waits for them, and re-layouts  4.45 us (2%)
    pallas_call x2, Pallas kernels, reduce_scatter(): pl.pallas_call(functools.partial(reduce_kernel, lines, crosses, paired),...  103 us
    pallas_call x2, Pallas kernels, gather(): pl.pallas_call(functools.partial(gather_kernel, lines, crosses, tuple(pai...  85.5 us
    dot_general x4, matrix products, contract_last(): lax.dot_general(left, right, (((1,), (1,)), ((), ())), preferred_element_...  9.58 us
    dot_general x4, matrix products, contract_first(): lax.dot_general(left, right, (((0,), (0,)), ((), ())), preferred_element_...  7.97 us
    concatenate x1, other arithmetic, body(): jnp.concatenate([term_value, term_output], axis=1).astype(jnp.bfloat16)  7.86 us
    dot_general x1, matrix products, body(): pulled = jnp.dot(grad_rows, output_full, preferred_element_type=jnp.float32)  5.04 us

profile of v1, /device:TPU:0, one launch (start us, length us, event | category | flops | bytes accessed | tf_op | source)
XLA Modules:
  0.0 236.5 jit_solution(17960128759725855189)
XLA Ops:
  0.6 0.0 copy-start
  0.7 0.8 fusion.25
  1.5 0.7 fusion.24
  2.2 0.7 bitcast_select_fusion
  2.9 0.7 bitcast_select_fusion.1
  3.6 65.7 %shard_map.154 = (bf16[4096,128]{1,0:T(8,128)(2,1)}, bf16[4096,512]{1,0:T(8,128)(2,1)}, bf16[4096,512]{1,0:T(8,128)(2,1)}) custom-call(bf16[256,128]{1,0:T(8,128)(2,1)} %bitcast.71, bf16[256,512]{1,0:T(8,128)(2,1)} %refs_1_.1, bf16[256,512]{1,0:T(8,128)(2,1)} %refs_2_.1), custom_call_target="tpu_custom_call" | custom-call | tf_op jit(solution)/shard_map/pallas_call | solution.py:255
  69.3 0.0 copy-done
  69.3 3.5 %fusion.15 = f32[512,256]{1,0:T(8,128)S(1)} fusion(bf16[4096,512]{1,0:T(8,128)(2,1)} %get-tuple-element.10, bf16[1,256,4096]{2,1,0:T(8,128)(2,1)S(1)} %copy-done), kind=kOutput, calls=%fused_computation.29 | convolution fusion | flops 1073741824 | bytes 6815744 | tf_op jit(solution)/shard_map/dot_general | solution.py:483
  72.8 0.7 copy.34.refs_0_
  73.6 0.0 copy-start.4
  73.6 0.0 copy-start.6
  73.6 0.0 copy-start.7
  73.6 5.0 %fusion.12 = f32[512,256]{1,0:T(8,128)} fusion(bf16[4096,512]{1,0:T(8,128)(2,1)} %get-tuple-element.11, bf16[1,256,4096]{2,1,0:T(8,128)(2,1)} %param.21), kind=kOutput, calls=%fused_computation.26 | convolution fusion | flops 1073741824 | bytes 6815744 | tf_op jit(solution)/shard_map/dot_general | solution.py:509
  78.6 19.8 %shard_map.155 = bf16[4096,128]{1,0:T(8,128)(2,1)} custom-call(bf16[256,128]{1,0:T(8,128)(2,1)} %copy.34.refs_0_), custom_call_target="tpu_custom_call" | custom-call | tf_op jit(solution)/shard_map/pallas_call | solution.py:255
  98.4 0.0 copy-done.4
  98.4 0.0 copy-done.6
  98.4 0.0 copy-done.7
  98.4 1.2 fusion.29
  99.6 0.0 copy-start.1
  99.6 0.0 copy-start.5
  99.7 0.6 exponential_reduce_fusion
  100.3 0.0 copy-start.2
  100.3 0.6 copy-done.1
  100.9 0.8 fusion.17
  101.7 0.0 copy-done.5
  101.7 0.1 multiply_reduce_fusion
  101.8 0.8 copy-done.2
  102.6 2.6 %fusion.6 = bf16[1,256,4096]{2,1,0:T(8,128)(2,1)} fusion(bf16[256,512]{0,1:T(8,128)(2,1)S(1)} %bitcast.67, bf16[4096,512]{1,0:T(8,128)(2,1)S(1)} %copy-done.2), kind=kOutput, calls=%fused_computation.13 | convolution fusion | flops 1074790400 | bytes 6553600 | tf_op jit(solution)/shard_map/dot_general | solution.py:443
  105.2 0.9 fusion.5
  106.1 0.7 convolution_convert_fusion.4
  106.9 1.4 fusion.19
  108.3 0.7 fusion.8
  109.0 1.5 pad_maximum_fusion.1.x_ref
  110.5 24.4 %shard_map.156 = bf16[256,256]{1,0:T(8,128)(2,1)} custom-call(bf16[4096,256]{1,0:T(8,128)(2,1)} %pad_maximum_fusion.1.x_ref), custom_call_target="tpu_custom_call" | custom-call | tf_op jit(solution)/shard_map/pallas_call | solution.py:416
  134.9 1.5 slice_bitcast_fusion
  136.4 0.1 copy.38
  136.6 4.8 %fusion.7 = bf16[1,256,4096]{2,1,0:T(8,128)(2,1)} fusion(bf16[256,512]{0,1:T(8,128)(2,1)S(1)} %bitcast.65, bf16[4096,512]{1,0:T(8,128)(2,1)} %get-tuple-element.10), kind=kOutput, calls=%fused_computation.14 | convolution fusion | flops 1074790400 | bytes 6553600 | tf_op jit(solution)/shard_map/dot_general | solution.py:443
  141.4 0.0 copy-start.3
  141.4 3.3 %fusion = bf16[4096,512]{1,0:T(8,128)(2,1)} fusion(bf16[256,512]{0,1:T(8,128)(2,1)S(1)} %bitcast.66, bf16[1,256,4096]{2,1,0:T(8,128)(2,1)S(1)} %copy-done), kind=kOutput, calls=%fused_computation.3 | convolution fusion | flops 1075838976 | bytes 6553600 | tf_op jit(solution)/shard_map/dot_general | solution.py:449
  144.7 0.0 copy-done.3
  144.7 3.3 %fusion.1 = bf16[4096,512]{1,0:T(8,128)(2,1)} fusion(bf16[256,512]{0,1:T(8,128)(2,1)S(1)} %bitcast.68, bf16[1,256,4096]{2,1,0:T(8,128)(2,1)S(1)} %copy-done.3), kind=kOutput, calls=%fused_computation.4 | convolution fusion | flops 1075838976 | bytes 6553600 | tf_op jit(solution)/shard_map/dot_general | solution.py:449
  148.0 7.9 %pad_maximum_fusion.x_ref = bf16[4096,1024]{1,0:T(8,128)(2,1)} fusion(bf16[4096,512]{1,0:T(8,128)(2,1)} %fusion.1, bf16[4096,512]{1,0:T(8,128)(2,1)} %fusion), kind=kLoop, calls=%fused_computation | loop fusion | flops 16777216 | bytes 16777216 | tf_op jit(solution)/shard_map/concatenate | solution.py:535
  155.8 78.4 %shard_map.157 = f32[256,1024]{1,0:T(8,128)} custom-call(bf16[4096,1024]{1,0:T(8,128)(2,1)} %pad_maximum_fusion.x_ref), custom_call_target="tpu_custom_call" | custom-call | tf_op jit(solution)/shard_map/pallas_call | solution.py:416
  234.2 2.2 fusion.28
  (5 shorter events, 0.1 us)
Async XLA Ops:
  0.6 68.6 %copy-start = (bf16[1,256,4096]{2,1,0:T(8,128)(2,1)S(1)}, bf16[1,256,4096]{2,1,0:T(8,128)(2,1)}, u32[]{:S(2)}) copy-start(bf16[1,256,4096]{2,1,0:T(8,128)(2,1)} %param.11) | copy-start | bytes 6291460
  73.6 24.8 %copy-start.4 = (bf16[4096,128]{1,0:T(8,128)(2,1)S(1)}, bf16[4096,128]{1,0:T(8,128)(2,1)}, u32[]{:S(2)}) copy-start(bf16[4096,128]{1,0:T(8,128)(2,1)} %get-tuple-element.9) | copy-start | bytes 3145732
  73.6 24.8 %copy-start.6 = (bf16[1,256,128]{2,1,0:T(8,128)(2,1)S(1)}, bf16[1,256,128]{2,1,0:T(8,128)(2,1)}, u32[]{:S(2)}) copy-start(bf16[1,256,128]{2,1,0:T(8,128)(2,1)} %param.12) | copy-start | bytes 196612
  73.6 24.8 %copy-start.7 = (s32[1,256]{1,0:T(1,128)S(1)}, s32[1,256]{1,0:T(1,128)}, u32[]{:S(2)}) copy-start(s32[1,256]{1,0:T(1,128)} %param.14) | copy-start | bytes 3076
  99.6 1.2 copy-start.1
  99.6 2.0 copy-start.5
  100.3 2.3 copy-start.2
  141.4 3.3 %copy-start.3 = (bf16[1,256,4096]{2,1,0:T(8,128)(2,1)S(1)}, bf16[1,256,4096]{2,1,0:T(8,128)(2,1)}, u32[]{:S(2)}) copy-start(bf16[1,256,4096]{2,1,0:T(8,128)(2,1)} %param.21) | copy-start | bytes 6291460

commit v2 on v1

--- a/solution.py
+++ b/solution.py
@@ -269,156 +269,196 @@
     )(*arrays)
 
 
-def reduce_kernel(lines, crosses, paired, x_ref, out_ref, total, core_in, mate_in, cross_in,
-                  line_in, last_in, sems):
+class Share:
+    def __init__(self, here, paired, source, out_ref, scratch):
+        self.here, self.paired, self.source, self.out = here, paired, source, out_ref
+        self.sent, self.total, self.core_in, self.mate_in, self.cross_in, self.line_in = scratch[:6]
+        self.last_in, self.sems = scratch[6:]
+        lines, self.crosses = here.lines, here.crosses
+        pieces = lines * self.crosses
+        self.rows = rows = out_ref.shape[0]
+        self.alone = alone = rows // 4 if paired else 0
+        self.carried = carried = rows - alone
+        self.base = [k * pieces for k in range(6)]
+        self.zs0 = 6 * pieces
+        self.zr0, self.fs = self.zs0 + lines, self.zs0 + 3 * lines
+        self.first = pl.ds(0, rows)
+        if paired:
+            self.first = pl.ds(pl.multiple_of(alone * here.side, 16), carried)
+            self.mine = pl.ds(pl.multiple_of(carried * here.side, 16), alone)
+            self.theirs = pl.ds(pl.multiple_of(carried * (1 - here.side), 16), alone)
+
+    def move(self, src, dst, send, recv, device):
+        return pltpu.make_async_remote_copy(
+            src_ref=src, dst_ref=dst, send_sem=self.sems.at[send], recv_sem=self.sems.at[recv],
+            device_id=device, device_id_type=MESH,
+        )
+
+    def slot(self, p, q):
+        return p * self.crosses + q
+
+    def term(self, p, q, c):
+        start = pl.multiple_of(((p * self.crosses + q) * 2 + c) * self.rows, self.rows)
+        if len(self.source) == 1:
+            return self.source[0][pl.ds(start, self.rows)]
+        acts, grads = self.source
+        return contract_first(acts[:, pl.ds(start, self.rows)], grads[...]).astype(jnp.bfloat16)
+
+    def to_core(self, p, q):
+        k = self.slot(p, q)
+        return self.move(self.sent.at[k], self.core_in.at[k], self.base[0] + k,
+                         self.base[1] + k, self.here.at(c=1 - self.here.c))
+
+    def to_mate(self, p, q):
+        k = self.slot(p, q)
+        return self.move(self.total.at[k, self.theirs], self.mate_in.at[k], self.base[2] + k,
+                         self.base[3] + k, self.here.at(dp=self.here.mate))
+
+    def across(self, p, q):
+        k = self.slot(p, self.here.b)
+        return self.move(self.total.at[self.slot(p, q), self.first], self.cross_in.at[k],
+                         self.base[4] + self.slot(p, q), self.base[5] + k, self.here.at(b=q))
+
+    def crossed(self, p, q):
+        k = self.slot(p, q)
+        return self.move(self.total.at[k, self.first], self.cross_in.at[k],
+                         self.base[4] + k, self.base[5] + k, self.here.at(b=q))
+
+    def along(self, p, step):
+        k = 2 * p + (0 if step > 0 else 1)
+        return self.move(self.total.at[self.slot(p, self.here.b), self.first],
+                         self.line_in.at[k], self.zs0 + p, self.zr0 + k,
+                         self.here.at(a=self.here.a + step))
+
+    def final(self):
+        k = self.slot(self.here.a, self.here.b)
+        return self.move(self.total.at[k, self.first], self.last_in, self.fs, self.fs + 1,
+                         self.here.at(dp=self.here.mate))
+
+    def begin(self, p, q):
+        self.sent[self.slot(p, q)] = self.term(p, q, 1 - self.here.c)
+        self.to_core(p, q).start()
+
+    def join(self, p, q):
+        k = self.slot(p, q)
+        self.total[k] = self.term(p, q, self.here.c)
+        self.to_core(p, q).wait_recv()
+        self.total[k] = self.total[k] + self.core_in[k]
+        if self.paired:
+            self.to_mate(p, q).start()
+
+    def cross(self, p, q, leave):
+        k = self.slot(p, q)
+        if self.paired:
+            self.to_mate(p, q).wait_recv()
+            self.total[k, self.mine] = self.total[k, self.mine] + self.mate_in[k]
+        if leave:
+            self.across(p, q).start()
+
+    def run(self, p, step):
+        here, k, first = self.here, self.slot(p, self.here.b), self.first
+        for q in here.others():
+            self.crossed(p, q).wait_recv()
+            self.total[k, first] = self.total[k, first] + self.cross_in[self.slot(p, q)]
+
+        def add(side):
+            self.along(p, 1 if side == 0 else -1).wait_recv()
+            self.total[k, first] = self.total[k, first] + self.line_in[2 * p + side]
+
+        if step >= 0:
+            pl.when(here.a > 0)(lambda: add(0))
+        if step <= 0:
+            pl.when(here.a < here.lines - 1)(lambda: add(1))
+        if step != 0:
+            self.along(p, step).start()
+        elif self.paired:
+            self.final().start()
+
+    def finish(self):
+        here, kind = self.here, self.out.dtype
+        k = self.slot(here.a, here.b)
+        if not self.paired:
+            self.out[...] = self.total[k].astype(kind)
+            return
+        alone, carried = self.alone, self.carried
+        middle = carried - alone
+        self.final().wait_recv()
+        self.out[self.mine] = self.total[k, self.mine].astype(kind)
+        their_at = pl.multiple_of(middle * (1 - here.side), 16)
+        self.out[self.theirs] = self.last_in[pl.ds(their_at, alone)].astype(kind)
+        shared_at = pl.multiple_of(alone * here.side, 16)
+        self.out[pl.ds(alone, middle)] = self.total[k, pl.ds(alone, middle)].astype(
+            kind
+        ) + self.last_in[pl.ds(shared_at, middle)].astype(kind)
+        self.final().wait_send()
+
+    def drain(self):
+        here = self.here
+        for p in range(here.lines):
+            for q in range(self.crosses):
+                self.to_core(p, q).wait_send()
+                if self.paired:
+                    self.to_mate(p, q).wait_send()
+            for q in here.others():
+                self.across(p, q).wait_send()
+            pl.when(p > here.a)(lambda p=p: self.along(p, 1).wait_send())
+            pl.when(p < here.a)(lambda p=p: self.along(p, -1).wait_send())
+
+
+def reduce_kernel(lines, crosses, forms, *refs):
     here = Place(lines, crosses)
-    pieces = lines * crosses
-    rows = out_ref.shape[0]
-    carried, alone = split_rows(rows) if paired else (rows, 0)
-    cs0, cr0, ys0, yr0, xs0, xr0 = (k * pieces for k in range(6))
-    zs0 = 6 * pieces
-    zr0, fs, fr = zs0 + lines, zs0 + 3 * lines, zs0 + 3 * lines + 1
-    first = pl.ds(pl.multiple_of(alone * here.side, 16), carried) if paired else pl.ds(0, rows)
-    mine = pl.ds(pl.multiple_of(carried * here.side, 16), alone)
-    theirs = pl.ds(pl.multiple_of(carried * (1 - here.side), 16), alone)
-
-    def move(src, dst, send, recv, device):
-        return pltpu.make_async_remote_copy(
-            src_ref=src, dst_ref=dst, send_sem=sems.at[send], recv_sem=sems.at[recv],
-            device_id=device, device_id_type=MESH,
-        )
-
-    def slot(p, q):
-        return p * crosses + q
-
-    def piece(p, q, c):
-        return pl.ds(pl.multiple_of(((p * crosses + q) * 2 + c) * rows, 16), rows)
-
-    def to_core(p, q):
-        k = slot(p, q)
-        return move(x_ref.at[piece(p, q, 1 - here.c)], core_in.at[k], cs0 + k, cr0 + k,
-                    here.at(c=1 - here.c))
-
-    def to_mate(p, q):
-        k = slot(p, q)
-        return move(total.at[k, theirs], mate_in.at[k], ys0 + k, yr0 + k,
-                    here.at(dp=here.mate))
-
-    def across(p, q):
-        return move(total.at[slot(p, q), first], cross_in.at[slot(p, here.b)],
-                    xs0 + slot(p, q), xr0 + slot(p, here.b), here.at(b=q))
-
-    def crossed(p, q):
-        return move(total.at[slot(p, q), first], cross_in.at[slot(p, q)],
-                    xs0 + slot(p, q), xr0 + slot(p, q), here.at(b=q))
-
-    def along(p, step):
-        k = 2 * p + (0 if step > 0 else 1)
-        return move(total.at[slot(p, here.b), first], line_in.at[k], zs0 + p, zr0 + k,
-                    here.at(a=here.a + step))
-
-    def final():
-        return move(total.at[slot(here.a, here.b), first], last_in, fs, fr,
-                    here.at(dp=here.mate))
-
-    here.greet(paired)
-    here.await_greetings(paired)
-    order = [(t, q) for t in range(lines - 1, -1, -1) for q in here.others() + [here.b]]
-    for t, q in order:
-        for p, _, ok in here.ring(t):
-            only(ok, lambda p=p, q=q: to_core(p, q).start())
-    for t, q in order:
-        for p, _, ok in here.ring(t):
-
-            def join(p=p, q=q):
-                k = slot(p, q)
-                to_core(p, q).wait_recv()
-                total[k] = x_ref[piece(p, q, here.c)] + core_in[k]
-                if paired:
-                    to_mate(p, q).start()
-
-            only(ok, join)
+    refs, sources = list(refs), []
+    for inputs, _ in forms:
+        sources.append(refs[:inputs])
+        refs = refs[inputs:]
+    outs, refs = refs[: len(forms)], refs[len(forms) :]
+    shares = [
+        Share(here, paired, sources[k], outs[k], refs[8 * k : 8 * k + 8])
+        for k, (_, paired) in enumerate(forms)
+    ]
+    any_pair = any(paired for _, paired in forms)
+    here.greet(any_pair)
+    here.await_greetings(any_pair)
+
+    def each(t, action):
+        if 0 <= t < lines:
+            for p, step, ok in here.ring(t):
+
+                def apply(p=p, step=step):
+                    for share in shares:
+                        action(share, p, step)
+
+                only(ok, apply)
+
     for t in range(lines - 1, -1, -1):
+        for q in here.others() + [here.b]:
+            each(t, lambda share, p, step, q=q: share.begin(p, q))
+    for t in range(lines - 1, -3, -1):
+        for q in here.others() + [here.b]:
+            each(t, lambda share, p, step, q=q: share.join(p, q))
         for q in here.others():
-            for p, _, ok in here.ring(t):
-
-                def cross(p=p, q=q):
-                    k = slot(p, q)
-                    if paired:
-                        to_mate(p, q).wait_recv()
-                        total[k, mine] = total[k, mine] + mate_in[k]
-                    across(p, q).start()
-
-                only(ok, cross)
-        for p, _, ok in here.ring(t):
-
-            def fold(p=p):
-                if paired:
-                    k = slot(p, here.b)
-                    to_mate(p, here.b).wait_recv()
-                    total[k, mine] = total[k, mine] + mate_in[k]
-
-            only(ok, fold)
-    for t in range(lines - 1, -1, -1):
-        for p, step, ok in here.ring(t):
-
-            def run(p=p, step=step):
-                k = slot(p, here.b)
-                for q in here.others():
-                    crossed(p, q).wait_recv()
-                    total[k, first] = total[k, first] + cross_in[slot(p, q)]
-
-                def add(side):
-                    along(p, 1 if side == 0 else -1).wait_recv()
-                    total[k, first] = total[k, first] + line_in[2 * p + side]
-
-                if step >= 0:
-                    pl.when(here.a > 0)(lambda: add(0))
-                if step <= 0:
-                    pl.when(here.a < lines - 1)(lambda: add(1))
-                if step != 0:
-                    along(p, step).start()
-
-            only(ok, run)
-
-    k = slot(here.a, here.b)
-    if paired:
-        final().start()
-        final().wait_recv()
-        out_ref[mine] = total[k, mine].astype(out_ref.dtype)
-        their_at = pl.multiple_of(alone * (1 - here.side) * 0 + (carried - alone) * (1 - here.side), 16)
-        out_ref[theirs] = last_in[pl.ds(their_at, alone)].astype(out_ref.dtype)
-        middle = carried - alone
-        shared_at = pl.multiple_of(alone * here.side, 16)
-        out_ref[pl.ds(alone, middle)] = total[k, pl.ds(alone, middle)].astype(
-            out_ref.dtype
-        ) + last_in[pl.ds(shared_at, middle)].astype(out_ref.dtype)
-        final().wait_send()
-    else:
-        out_ref[...] = total[k].astype(out_ref.dtype)
-    for p in range(lines):
-        for q in range(crosses):
-            to_core(p, q).wait_send()
-            if paired:
-                to_mate(p, q).wait_send()
-        for q in here.others():
-            across(p, q).wait_send()
-        pl.when(p > here.a)(lambda p=p: along(p, 1).wait_send())
-        pl.when(p < here.a)(lambda p=p: along(p, -1).wait_send())
-
-
-def reduce_scatter(x, paired, size, out_dtype, collective_id):
+            each(t + 1, lambda share, p, step, q=q: share.cross(p, q, True))
+        each(t + 1, lambda share, p, step: share.cross(p, here.b, False))
+        each(t + 2, lambda share, p, step: share.run(p, step))
+    for share in shares:
+        share.finish()
+    for share in shares:
+        share.drain()
+
+
+def reduce_scatter(sources, paired, out_dtypes, size, collective_id):
     lines, crosses = layout(size)
     pieces = lines * crosses
-    rows, width = x.shape[0] // size, x.shape[1]
-    carried, alone = split_rows(rows) if paired else (rows, 16)
-    kind = x.dtype
-    return pl.pallas_call(
-        functools.partial(reduce_kernel, lines, crosses, paired),
-        out_shape=jax.ShapeDtypeStruct((rows, width), out_dtype),
-        in_specs=[pl.BlockSpec(memory_space=pltpu.VMEM)],
-        out_specs=pl.BlockSpec(memory_space=pltpu.VMEM),
-        scratch_shapes=[
+    kind = jnp.bfloat16
+    outs, scratch = [], []
+    for source, pair, out_dtype in zip(sources, paired, out_dtypes):
+        rows = source[0].shape[len(source) - 1] // size
+        width = source[-1].shape[1]
+        alone = rows // 4 if pair else 16
+        carried = rows - rows // 4 if pair else rows
+        outs.append(jax.ShapeDtypeStruct((rows, width), out_dtype))
+        scratch += [
+            pltpu.VMEM((pieces, rows, width), kind),
             pltpu.VMEM((pieces, rows, width), kind),
             pltpu.VMEM((pieces, rows, width), kind),
             pltpu.VMEM((pieces, alone, width), kind),
@@ -426,12 +466,20 @@
             pltpu.VMEM((2 * lines, carried, width), kind),
             pltpu.VMEM((carried, width), kind),
             pltpu.SemaphoreType.DMA((6 * pieces + 3 * lines + 2,)),
-        ],
+        ]
+    flat = [x for source in sources for x in source]
+    forms = tuple((len(source), pair) for source, pair in zip(sources, paired))
+    return pl.pallas_call(
+        functools.partial(reduce_kernel, lines, crosses, forms),
+        out_shape=outs,
+        in_specs=[pl.BlockSpec(memory_space=pltpu.VMEM)] * len(flat),
+        out_specs=[pl.BlockSpec(memory_space=pltpu.VMEM)] * len(outs),
+        scratch_shapes=scratch,
         compiler_params=pltpu.CompilerParams(
             collective_id=collective_id, has_side_effects=True,
-            vmem_limit_bytes=56 * 1024 * 1024,
+            vmem_limit_bytes=48 * 1024 * 1024,
         ),
-    )(x)
+    )(*flat)
 
 
 def expert_gates(scores, chosen, experts):
@@ -477,14 +525,12 @@
     output_gate = expert_gates(output_scores[0], output_experts[0], experts)
     size = lax.axis_size("seq")
     pair_count = lax.axis_size("dp")
-    keys_all, value_full, output_full = gather(
-        [own_keys, value_panels, output_panels], [False, True, True], size, 0
-    )
+    value_full, keys_all = gather([value_panels, own_keys], [True, False], size, 0)
     projection = jnp.dot(tok_block, value_full, preferred_element_type=jnp.float32)
     value_vec = jnp.sum(
         projection.reshape(tok_rows, experts, head_size) * value_gate[:, :, None], axis=1
     ).astype(jnp.bfloat16)
-    (values_all,) = gather([value_vec], [False], size, 1)
+    values_all, output_full = gather([value_vec, output_panels], [False, True], size, 1)
     length = keys_all.shape[0]
     score_scale = head_size ** (-0.5)
     query_index = lax.axis_index("seq") * tok_rows + lax.iota(jnp.int32, tok_rows)
@@ -518,9 +564,12 @@
     ).astype(jnp.bfloat16)
     key_term = contract_first(dscores, query_block) * score_scale
     value_term = contract_first(prob_low, dattended)
-    own_sums = reduce_scatter(
-        jnp.concatenate([key_term, value_term], axis=1).astype(jnp.bfloat16),
-        False, size, jnp.bfloat16, 2,
+    own_sums, grad_output = reduce_scatter(
+        [
+            (jnp.concatenate([key_term, value_term], axis=1).astype(jnp.bfloat16),),
+            (grad_rows, expanded),
+        ],
+        [False, True], [jnp.bfloat16, jnp.float32], size, 2,
     )
     grad_keys, dvalue = own_sums[:, :head_size], own_sums[:, head_size:]
     value_grad = (
@@ -529,21 +578,18 @@
         .astype(jnp.bfloat16)
     )
     grad_tokens = contract_last(value_grad, value_full).astype(jnp.bfloat16)
-    term_value = contract_first(tok_block, value_grad)
-    term_output = contract_first(grad_rows, expanded)
-    summed = reduce_scatter(
-        jnp.concatenate([term_value, term_output], axis=1).astype(jnp.bfloat16),
-        True, size, jnp.float32, 3,
+    (grad_value,) = reduce_scatter(
+        [(tok_block, value_grad)], [True], [jnp.float32], size, 3
     )
     if pair_count > 2:
-        summed = lax.psum(summed * 0.5, "dp")
+        grad_value, grad_output = lax.psum((grad_value * 0.5, grad_output * 0.5), "dp")
     return (
         layer_output[None],
         grad_tokens[None],
         grad_queries[None],
         grad_keys[None],
-        summed[:, :panel_width],
-        summed[:, panel_width:],
+        grad_value,
+        grad_output,
     )
 
 

time: 237 us -> 203 us (0.86)
  Pallas kernels: 188 us -> 161 us
  other arithmetic: 14.7 us -> 9.11 us
  matrix products: 28.3 us -> 23.5 us
  local copies, waits for them, and re-layouts: 4.45 us -> 8.02 us
    pallas_call x2, Pallas kernels: 103 us -> 76.6 us  [reduce_scatter(): pl.pallas_call(functools.partial(reduce_kernel, lines, crosses, forms), o...]
    concatenate x1 -> x0, other arithmetic: 7.86 us -> none  [body(): jnp.concatenate([term_value, term_output], axis=1).astype(jnp.bfloat16)]
    dot_general x4 -> x2, matrix products: 7.97 us -> 1.43 us  [contract_first(): lax.dot_general(left, right, (((0,), (0,)), ((), ())), preferred_element_...]
    unnamed x16 -> x30, local copies, waits for them, and re-layouts: 1.39 us -> 4.18 us
    dot_general x1, matrix products: 0.8 us -> 3.29 us  [body(): jnp.dot(prob_low, values_all, preferred_element_type=jnp.float32)]
where the time goes in v2:
time: 203 us; the launch traced here: 202 us
  Pallas kernels  161 us (79%)
  matrix products  23.5 us (12%)
  other arithmetic  9.11 us (4%)
  local copies, waits for them, and re-layouts  8.02 us (4%)
    pallas_call x2, Pallas kernels, gather(): pl.pallas_call(functools.partial(gather_kernel, lines, crosses, tuple(pai...  84 us
    pallas_call x2, Pallas kernels, reduce_scatter(): pl.pallas_call(functools.partial(reduce_kernel, lines, crosses, forms), o...  76.6 us
    dot_general x4, matrix products, contract_last(): lax.dot_general(left, right, (((1,), (1,)), ((), ())), preferred_element_...  9.71 us
    dot_general x1, matrix products, body(): jnp.dot(tok_block, value_full, preferred_element_type=jnp.float32)  4.23 us
    unnamed x30, local copies, waits for them, and re-layouts  4.18 us

profile of v2, /device:TPU:0, one launch (start us, length us, event | category | flops | bytes accessed | tf_op | source)
XLA Modules:
  0.0 202.2 jit_solution(8108663999587346942)
XLA Ops:
  0.6 0.0 copy-start
  0.7 0.7 fusion.17
  1.4 0.7 fusion.16
  2.1 0.7 bitcast_select_fusion.1
  2.8 0.7 bitcast_select_fusion
  3.5 0.1 copy.39
  3.6 0.0 copy-start.8
  3.6 0.8 copy.38
  4.4 42.8 %shard_map.154 = (bf16[4096,512]{1,0:T(8,128)(2,1)}, bf16[4096,128]{1,0:T(8,128)(2,1)}) custom-call(bf16[256,512]{1,0:T(8,128)(2,1)} %refs_0_.1, bf16[256,128]{1,0:T(8,128)(2,1)} %bitcast.71), custom_call_target="tpu_custom_call" | custom-call | tf_op jit(solution)/shard_map/pallas_call | solution.py:255
  47.2 0.0 copy-start.10
  47.2 0.0 copy-start.12
  47.2 4.2 %fusion.20 = f32[512,256]{1,0:T(8,128)S(1)} fusion(bf16[4096,512]{1,0:T(8,128)(2,1)} %get-tuple-element.13, bf16[1,256,4096]{2,1,0:T(8,128)(2,1)} %param.11), kind=kOutput, calls=%fused_computation.46 | convolution fusion | flops 1073741824 | bytes 6815744 | tf_op jit(solution)/shard_map/dot_general | solution.py:529
  51.5 0.2 copy.40
  51.7 0.0 copy-done.8
  51.7 1.0 multiply_reduce_fusion.1.refs_0_
  52.8 0.0 copy-done
  52.8 0.0 copy-done.10
  52.8 0.0 copy-done.12
  52.8 1.2 fusion.24
  54.0 0.0 copy-start.3
  54.0 2.0 copy-done.3
  56.0 0.0 copy-start.1
  56.0 0.6 exponential_reduce_fusion
  56.6 41.2 %shard_map.155 = (bf16[4096,128]{1,0:T(8,128)(2,1)}, bf16[4096,512]{1,0:T(8,128)(2,1)}) custom-call(bf16[256,128]{1,0:T(8,128)(2,1)} %multiply_reduce_fusion.1.refs_0_, bf16[256,512]{1,0:T(8,128)(2,1)} %refs_1_.1), custom_call_target="tpu_custom_call" | custom-call | tf_op jit(solution)/shard_map/pallas_call | solution.py:255
  97.8 3.3 %fusion.9 = f32[256,128]{0,1:T(8,128)S(1)} fusion(bf16[4096,128]{1,0:T(8,128)(2,1)} %get-tuple-element.14, f32[256,4096]{0,1:T(8,128)} %copy-done.3, f32[256]{0:T(256)S(1)} %log_add_fusion), kind=kOutput, calls=%fused_computation.22 | convolution fusion | flops 270598144 | bytes 5374976 | tf_op jit(solution)/shard_map/dot_general | solution.py:546
  101.1 0.0 copy-start.7
  101.2 0.8 copy.41
  101.9 0.0 copy-done.1
  101.9 3.5 %fusion.18 = f32[512,256]{1,0:T(8,128)S(1)} fusion(bf16[4096,512]{1,0:T(8,128)(2,1)} %get-tuple-element.15, bf16[1,256,4096]{2,1,0:T(8,128)(2,1)S(1)} %copy-done.1), kind=kOutput, calls=%fused_computation.44 | convolution fusion | flops 1073741824 | bytes 6815744 | tf_op jit(solution)/shard_map/dot_general | solution.py:555
  105.4 0.0 copy-done.7
  105.4 1.0 copy.42
  106.4 0.0 copy-start.6
  106.4 2.3 %multiply_reduce_fusion = (bf16[256,128]{1,0:T(8,128)(2,1)}, bf16[256,4,128]{2,1,0:T(4,128)(2,1)S(1)}) fusion(f32[256,4,128]{2,1,0:T(4,128)} %copy.42, f32[256,4]{1,0:T(8,128)} %copy.38, f32[256,128]{1,0:T(8,128)} %copy.41), kind=kLoop, calls=%fused_computation.26 | loop fusion | flops 491520 | bytes 987136 | tf_op jit(solution)/shard_map/reduce_sum | solution.py:556
  108.7 0.9 copy.43
  109.7 0.0 copy-start.4
  109.7 1.1 multiply_reduce_fusion.2
  110.8 5.0 %fusion.4 = bf16[1,256,4096]{2,1,0:T(8,128)(2,1)} fusion(bf16[4096,512]{1,0:T(8,128)(2,1)} %get-tuple-element.15, bf16[32,8,4,128]{3,2,1,0:T(4,128)(2,1)S(1)} %bitcast.65), kind=kOutput, calls=%fused_computation.8 | convolution fusion | flops 1074790400 | bytes 6553600 | tf_op jit(solution)/shard_map/dot_general | solution.py:491
  115.8 0.0 copy-done.6
  115.8 0.0 copy-done.4
  115.9 0.9 fusion.3
  116.7 0.0 copy-start.11
  116.7 0.7 convolution_convert_fusion.2
  117.5 0.5 copy-done.11
  118.0 1.4 fusion.11
  119.3 0.7 fusion.6
  120.0 0.0 copy-start.9
  120.1 0.0 copy-start.5
  120.1 0.2 pad_maximum_fusion.refs_0_
  120.3 41.2 %shard_map.156 = (bf16[256,256]{1,0:T(8,128)(2,1)S(1)}, f32[256,512]{1,0:T(8,128)S(1)}) custom-call(bf16[4096,256]{1,0:T(8,128)(2,1)S(1)} %pad_maximum_fusion.refs_0_, bf16[256,4096]{1,0:T(8,128)(2,1)S(1)} %bitcast.61, bf16[256,512]{1,0:T(8,128)(2,1)S(1)} %bitcast.63), custom_call_target="tpu_custom_call" | custom-call | tf_op jit(solution)/shard_map/pallas_call | solution.py:472
  161.5 0.0 copy-start.2
  161.5 0.6 slice_bitcast_fusion
  162.2 0.0 copy-done.9
  162.2 0.3 multiply_convert_fusion
  162.5 0.0 copy-done.5
  162.5 2.6 %fusion.5 = bf16[1,256,4096]{2,1,0:T(8,128)(2,1)} fusion(bf16[4096,512]{1,0:T(8,128)(2,1)S(1)} %copy-done.5, bf16[32,8,4,128]{3,2,1,0:T(4,128)(2,1)S(1)} %bitcast.67), kind=kOutput, calls=%fused_computation.9 | convolution fusion | flops 1074790400 | bytes 6553600 | tf_op jit(solution)/shard_map/dot_general | solution.py:491
  165.2 0.0 copy-done.2
  165.2 35.4 %shard_map.157 = f32[256,512]{1,0:T(8,128)S(1)} custom-call(bf16[256,4096]{1,0:T(8,128)(2,1)S(1)} %bitcast.62, bf16[256,512]{1,0:T(8,128)(2,1)S(1)} %bitcast.64), custom_call_target="tpu_custom_call" | custom-call | tf_op jit(solution)/shard_map/pallas_call | solution.py:472
  200.6 0.8 copy.60
  201.4 0.8 copy.61
  (4 shorter events, 0.1 us)
Async XLA Ops:
  0.6 52.1 %copy-start = (bf16[1,256,128]{2,1,0:T(8,128)(2,1)S(1)}, bf16[1,256,128]{2,1,0:T(8,128)(2,1)}, u32[]{:S(2)}) copy-start(bf16[1,256,128]{2,1,0:T(8,128)(2,1)} %param.12) | copy-start | bytes 196612
  3.6 48.1 %copy-start.8 = (f32[256,4]{1,0:T(8,128)}, f32[256,4]{1,0:T(8,128)S(1)}, u32[]{:S(2)}) copy-start(f32[256,4]{1,0:T(8,128)S(1)} %copy.39) | copy-start | bytes 12292
  47.2 5.5 %copy-start.10 = (bf16[4096,128]{1,0:T(8,128)(2,1)S(1)}, bf16[4096,128]{1,0:T(8,128)(2,1)}, u32[]{:S(2)}) copy-start(bf16[4096,128]{1,0:T(8,128)(2,1)} %get-tuple-element.12) | copy-start | bytes 3145732
  47.2 5.5 %copy-start.12 = (s32[1,256]{1,0:T(1,128)S(1)}, s32[1,256]{1,0:T(1,128)}, u32[]{:S(2)}) copy-start(s32[1,256]{1,0:T(1,128)} %param.14) | copy-start | bytes 3076
  54.0 2.0 copy-start.3
  56.0 45.9 %copy-start.1 = (bf16[1,256,4096]{2,1,0:T(8,128)(2,1)S(1)}, bf16[1,256,4096]{2,1,0:T(8,128)(2,1)}, u32[]{:S(2)}) copy-start(bf16[1,256,4096]{2,1,0:T(8,128)(2,1)} %param.21) | copy-start | bytes 6291460
  101.1 4.3 %copy-start.7 = (f32[256,128]{0,1:T(8,128)}, f32[256,128]{0,1:T(8,128)S(1)}, u32[]{:S(2)}) copy-start(f32[256,128]{0,1:T(8,128)S(1)} %fusion.9) | copy-start | bytes 393220
  106.4 9.4 %copy-start.6 = (bf16[4096,128]{1,0:T(8,128)(2,1)S(1)}, bf16[4096,128]{1,0:T(8,128)(2,1)}, u32[]{:S(2)}) copy-start(bf16[4096,128]{1,0:T(8,128)(2,1)} %get-tuple-element.14) | copy-start | bytes 3145732
  109.7 6.2 %copy-start.4 = (f32[256,4096]{0,1:T(8,128)S(1)}, f32[256,4096]{0,1:T(8,128)}, u32[]{:S(2)}) copy-start(f32[256,4096]{0,1:T(8,128)} %copy-done.3) | copy-start | bytes 12582916
  116.7 1.2 copy-start.11
  120.0 42.1 %copy-start.9 = (f32[256,4]{1,0:T(8,128)S(1)}, f32[256,4]{1,0:T(8,128)}, u32[]{:S(2)}) copy-start(f32[256,4]{1,0:T(8,128)} %copy-done.8) | copy-start | bytes 12292
  120.1 42.5 %copy-start.5 = (bf16[4096,512]{1,0:T(8,128)(2,1)S(1)}, bf16[4096,512]{1,0:T(8,128)(2,1)}, u32[]{:S(2)}) copy-start(bf16[4096,512]{1,0:T(8,128)(2,1)} %get-tuple-element.13) | copy-start | bytes 12582916
  161.5 3.7 %copy-start.2 = (bf16[1,256,4096]{2,1,0:T(8,128)(2,1)S(1)}, bf16[1,256,4096]{2,1,0:T(8,128)(2,1)}, u32[]{:S(2)}) copy-start(bf16[1,256,4096]{2,1,0:T(8,128)(2,1)} %param.11) | copy-start | bytes 6291460

commit v3 on v2

--- a/solution.py
+++ b/solution.py
@@ -257,14 +257,15 @@
         out_shape=[
             jax.ShapeDtypeStruct((size * x.shape[0],) + x.shape[1:], x.dtype) for x in arrays
         ],
-        in_specs=[pl.BlockSpec(memory_space=pl.ANY)] * count,
-        out_specs=[pl.BlockSpec(memory_space=pl.ANY)] * count,
+        in_specs=[pl.BlockSpec(memory_space=pltpu.VMEM)] * count,
+        out_specs=[pl.BlockSpec(memory_space=pltpu.VMEM)] * count,
         scratch_shapes=[
             pltpu.SemaphoreType.DMA((3 * lines + 6 * lines * crosses,)) for _ in range(count)
         ]
         + [pltpu.SemaphoreType.DMA((count,))],
         compiler_params=pltpu.CompilerParams(
-            collective_id=collective_id, has_side_effects=True
+            collective_id=collective_id, has_side_effects=True,
+            vmem_limit_bytes=32 * 1024 * 1024,
         ),
     )(*arrays)
 

time: 203 us -> 182 us (0.90)
  Pallas kernels: 161 us -> 138 us
  local copies, waits for them, and re-layouts: 8.02 us -> 13.2 us
  matrix products: 23.5 us -> 20.5 us
    pallas_call x2, Pallas kernels: 84 us -> 60.5 us  [gather(): pl.pallas_call(functools.partial(gather_kernel, lines, crosses, tuple(pai...]
    unnamed x30 -> x38, local copies, waits for them, and re-layouts: 4.18 us -> 8.35 us
    dot_general x1, matrix products: 3.29 us -> 0.8 us  [body(): jnp.dot(prob_low, values_all, preferred_element_type=jnp.float32)]
where the time goes in v3:
time: 182 us; the launch traced here: 181 us
  Pallas kernels  138 us (76%)
  matrix products  20.5 us (11%)
  local copies, waits for them, and re-layouts  13.2 us (7%)
  other arithmetic  8.41 us (5%)
    pallas_call x2, Pallas kernels, reduce_scatter(): pl.pallas_call(functools.partial(reduce_kernel, lines, crosses, forms), o...  77.7 us
    pallas_call x2, Pallas kernels, gather(): pl.pallas_call(functools.partial(gather_kernel, lines, crosses, tuple(pai...  60.5 us
    dot_general x4, matrix products, contract_last(): lax.dot_general(left, right, (((1,), (1,)), ((), ())), preferred_element_...  9.7 us
    unnamed x38, local copies, waits for them, and re-layouts  8.35 us
    dot_general x1, matrix products, body(): pulled = jnp.dot(grad_rows, output_full, preferred_element_type=jnp.float32)  4.28 us

profile of v3, /device:TPU:0, one launch (start us, length us, event | category | flops | bytes accessed | tf_op | source)
XLA Modules:
  0.0 181.2 jit_solution(1862891170707350973)
XLA Ops:
  0.6 0.0 copy-start
  0.7 0.7 fusion.17
  1.4 0.7 fusion.16
  2.1 0.7 bitcast_select_fusion.1
  2.8 0.7 bitcast_select_fusion
  3.5 0.1 copy.39
  3.6 0.0 copy-start.14
  3.6 0.8 copy.38
  4.4 0.9 copy-done.8
  5.4 0.8 copy-done.10
  6.2 31.2 %shard_map.154 = (bf16[4096,512]{1,0:T(8,128)(2,1)S(1)}, bf16[4096,128]{1,0:T(8,128)(2,1)S(1)}) custom-call(bf16[256,512]{1,0:T(8,128)(2,1)S(1)} %copy-done.8, bf16[256,128]{1,0:T(8,128)(2,1)S(1)} %bitcast.65), custom_call_target="tpu_custom_call" | custom-call | tf_op jit(solution)/shard_map/pallas_call | solution.py:255
  37.4 0.0 copy-start.1
  37.4 0.0 copy-start.6
  37.4 1.9 %copy-done.1 = bf16[4096,512]{1,0:T(8,128)(2,1)} copy-done((bf16[4096,512]{1,0:T(8,128)(2,1)}, bf16[4096,512]{1,0:T(8,128)(2,1)S(1)}, u32[]{:S(2)}) %copy-start.1) | copy-done | bytes 4194328
  39.3 2.9 %fusion.20 = f32[512,256]{1,0:T(8,128)S(1)} fusion(bf16[4096,512]{1,0:T(8,128)(2,1)S(1)} %get-tuple-element.13, bf16[1,256,4096]{2,1,0:T(8,128)(2,1)} %param.11), kind=kOutput, calls=%fused_computation.46 | convolution fusion | flops 1073741824 | bytes 6815744 | tf_op jit(solution)/shard_map/dot_general | solution.py:530
  42.2 0.2 copy.40
  42.5 0.0 copy-done.14
  42.5 0.4 multiply_reduce_fusion.1.refs_0_
  42.9 0.0 copy-done.6
  42.9 0.0 copy-done
  42.9 0.0 copy-done.16
  42.9 1.2 fusion.24
  44.1 0.0 copy-start.11
  44.1 0.0 copy-start.9
  44.1 0.0 copy-start.4
  44.2 0.6 exponential_reduce_fusion
  44.8 0.5 copy-done.9
  45.3 29.4 %shard_map.155 = (bf16[4096,128]{1,0:T(8,128)(2,1)S(1)}, bf16[4096,512]{1,0:T(8,128)(2,1)S(1)}) custom-call(bf16[256,128]{1,0:T(8,128)(2,1)S(1)} %multiply_reduce_fusion.1.refs_0_, bf16[256,512]{1,0:T(8,128)(2,1)S(1)} %copy-done.9), custom_call_target="tpu_custom_call" | custom-call | tf_op jit(solution)/shard_map/pallas_call | solution.py:255
  74.6 0.0 copy-start.3
  74.7 1.9 %copy-done.3 = bf16[4096,512]{1,0:T(8,128)(2,1)} copy-done((bf16[4096,512]{1,0:T(8,128)(2,1)}, bf16[4096,512]{1,0:T(8,128)(2,1)S(1)}, u32[]{:S(2)}) %copy-start.3) | copy-done | bytes 4194328
  76.6 0.0 copy-done.11
  76.6 0.8 fusion.9
  77.4 0.0 copy-start.13
  77.4 0.7 copy.41
  78.2 0.0 copy-done.4
  78.2 4.3 %fusion.18 = f32[512,256]{1,0:T(8,128)} fusion(bf16[4096,512]{1,0:T(8,128)(2,1)} %copy-done.3, bf16[1,256,4096]{2,1,0:T(8,128)(2,1)S(1)} %copy-done.4), kind=kOutput, calls=%fused_computation.44 | convolution fusion | flops 1073741824 | bytes 6815744 | tf_op jit(solution)/shard_map/dot_general | solution.py:556
  82.5 0.0 copy-done.13
  82.5 2.0 %copy.42 = f32[256,4,128]{2,1,0:T(4,128)} copy(f32[256,4,128]{0,2,1:T(8,128)} %bitcast.71) | data formatting | bytes 1048576 | tf_op jit(solution)/shard_map/reshape | solution.py:558
  84.5 2.2 %multiply_reduce_fusion = (bf16[256,128]{1,0:T(8,128)(2,1)}, bf16[256,4,128]{2,1,0:T(4,128)(2,1)S(1)}) fusion(f32[256,4,128]{2,1,0:T(4,128)} %copy.42, f32[256,4]{1,0:T(8,128)} %copy.38, f32[256,128]{1,0:T(8,128)} %copy.41), kind=kLoop, calls=%fused_computation.26 | loop fusion | flops 491520 | bytes 987136 | tf_op jit(solution)/shard_map/reduce_sum | solution.py:557
  86.7 0.9 copy.43
  87.7 0.0 copy-start.12
  87.7 1.1 multiply_reduce_fusion.2
  88.8 5.0 %fusion.4 = bf16[1,256,4096]{2,1,0:T(8,128)(2,1)} fusion(bf16[4096,512]{1,0:T(8,128)(2,1)} %copy-done.3, bf16[32,8,4,128]{3,2,1,0:T(4,128)(2,1)S(1)} %bitcast.66), kind=kOutput, calls=%fused_computation.8 | convolution fusion | flops 1074790400 | bytes 6553600 | tf_op jit(solution)/shard_map/dot_general | solution.py:492
  93.8 0.0 copy-done.12
  93.9 0.9 fusion.3
  94.7 0.0 copy-start.7
  94.7 0.7 convolution_convert_fusion.2
  95.5 0.5 copy-done.7
  96.0 1.4 fusion.11
  97.3 0.7 fusion.6
  98.0 0.0 copy-start.15
  98.1 0.0 copy-start.2
  98.1 0.2 pad_maximum_fusion.refs_0_
  98.3 41.7 %shard_map.156 = (bf16[256,256]{1,0:T(8,128)(2,1)S(1)}, f32[256,512]{1,0:T(8,128)S(1)}) custom-call(bf16[4096,256]{1,0:T(8,128)(2,1)S(1)} %pad_maximum_fusion.refs_0_, bf16[256,4096]{1,0:T(8,128)(2,1)S(1)} %bitcast.61, bf16[256,512]{1,0:T(8,128)(2,1)S(1)} %bitcast.63), custom_call_target="tpu_custom_call" | custom-call | tf_op jit(solution)/shard_map/pallas_call | solution.py:473
  140.0 0.0 copy-start.5
  140.0 0.6 slice_bitcast_fusion
  140.7 0.0 copy-done.15
  140.7 0.3 multiply_convert_fusion
  141.0 0.0 copy-done.2
  141.0 2.6 %fusion.5 = bf16[1,256,4096]{2,1,0:T(8,128)(2,1)} fusion(bf16[4096,512]{1,0:T(8,128)(2,1)S(1)} %copy-done.2, bf16[32,8,4,128]{3,2,1,0:T(4,128)(2,1)S(1)} %bitcast.68), kind=kOutput, calls=%fused_computation.9 | convolution fusion | flops 1074790400 | bytes 6553600 | tf_op jit(solution)/shard_map/dot_general | solution.py:492
  143.7 0.0 copy-done.5
  143.7 36.0 %shard_map.157 = f32[256,512]{1,0:T(8,128)S(1)} custom-call(bf16[256,4096]{1,0:T(8,128)(2,1)S(1)} %bitcast.62, bf16[256,512]{1,0:T(8,128)(2,1)S(1)} %bitcast.64), custom_call_target="tpu_custom_call" | custom-call | tf_op jit(solution)/shard_map/pallas_call | solution.py:473
  179.7 0.8 copy.60
  180.4 0.8 copy.61
  (7 shorter events, 0.1 us)
Async XLA Ops:
  0.6 42.3 %copy-start = (bf16[1,256,128]{2,1,0:T(8,128)(2,1)S(1)}, bf16[1,256,128]{2,1,0:T(8,128)(2,1)}, u32[]{:S(2)}) copy-start(bf16[1,256,128]{2,1,0:T(8,128)(2,1)} %param.12) | copy-start | bytes 196612
  3.6 38.8 %copy-start.14 = (f32[256,4]{1,0:T(8,128)}, f32[256,4]{1,0:T(8,128)S(1)}, u32[]{:S(2)}) copy-start(f32[256,4]{1,0:T(8,128)S(1)} %copy.39) | copy-start | bytes 12292
  4.4 0.9 copy-start.8
  5.4 0.8 copy-start.10
  37.4 1.9 %copy-start.1 = (bf16[4096,512]{1,0:T(8,128)(2,1)}, bf16[4096,512]{1,0:T(8,128)(2,1)S(1)}, u32[]{:S(2)}) copy-start(bf16[4096,512]{1,0:T(8,128)(2,1)S(1)} %get-tuple-element.13) | copy-start | bytes 12582916
  37.4 5.5 %copy-start.6 = (bf16[4096,128]{1,0:T(8,128)(2,1)}, bf16[4096,128]{1,0:T(8,128)(2,1)S(1)}, u32[]{:S(2)}) copy-start(bf16[4096,128]{1,0:T(8,128)(2,1)S(1)} %get-tuple-element.12) | copy-start | bytes 3145732
  39.3 3.6 %copy-start.16 = (s32[1,256]{1,0:T(1,128)S(1)}, s32[1,256]{1,0:T(1,128)}, u32[]{:S(2)}) copy-start(s32[1,256]{1,0:T(1,128)} %param.14) | copy-start | bytes 3076
  44.1 32.5 %copy-start.11 = (f32[256,4096]{0,1:T(8,128)}, f32[256,4096]{0,1:T(8,128)S(1)}, u32[]{:S(2)}) copy-start(f32[256,4096]{0,1:T(8,128)S(1)} %get-tuple-element.23) | copy-start | bytes 12582916
  44.1 1.1 copy-start.9
  44.1 34.0 %copy-start.4 = (bf16[1,256,4096]{2,1,0:T(8,128)(2,1)S(1)}, bf16[1,256,4096]{2,1,0:T(8,128)(2,1)}, u32[]{:S(2)}) copy-start(bf16[1,256,4096]{2,1,0:T(8,128)(2,1)} %param.21) | copy-start | bytes 6291460
  74.6 2.0 %copy-start.3 = (bf16[4096,512]{1,0:T(8,128)(2,1)}, bf16[4096,512]{1,0:T(8,128)(2,1)S(1)}, u32[]{:S(2)}) copy-start(bf16[4096,512]{1,0:T(8,128)(2,1)S(1)} %get-tuple-element.15) | copy-start | bytes 12582916
  77.4 5.0 %copy-start.13 = (f32[256,128]{0,1:T(8,128)}, f32[256,128]{0,1:T(8,128)S(1)}, u32[]{:S(2)}) copy-start(f32[256,128]{0,1:T(8,128)S(1)} %fusion.9) | copy-start | bytes 393220
  87.7 6.2 %copy-start.12 = (f32[256,4096]{0,1:T(8,128)S(1)}, f32[256,4096]{0,1:T(8,128)}, u32[]{:S(2)}) copy-start(f32[256,4096]{0,1:T(8,128)} %copy-done.11) | copy-start | bytes 12582916
  94.7 1.2 copy-start.7
  98.0 42.6 %copy-start.15 = (f32[256,4]{1,0:T(8,128)S(1)}, f32[256,4]{1,0:T(8,128)}, u32[]{:S(2)}) copy-start(f32[256,4]{1,0:T(8,128)} %copy-done.14) | copy-start | bytes 12292
  98.1 43.0 %copy-start.2 = (bf16[4096,512]{1,0:T(8,128)(2,1)S(1)}, bf16[4096,512]{1,0:T(8,128)(2,1)}, u32[]{:S(2)}) copy-start(bf16[4096,512]{1,0:T(8,128)(2,1)} %copy-done.1) | copy-start | bytes 12582916
  140.0 3.7 %copy-start.5 = (bf16[1,256,4096]{2,1,0:T(8,128)(2,1)S(1)}, bf16[1,256,4096]{2,1,0:T(8,128)(2,1)}, u32[]{:S(2)}) copy-start(bf16[1,256,4096]{2,1,0:T(8,128)(2,1)} %param.11) | copy-start | bytes 6291460
